TPU v7x, 32 devices: a whole 2x2x4 slice. The times are simulated.
32 devices in a mesh: parts: 1, ctx: 4 (over z), pb: 4 (over y, x), row: 2 (over core).
Axes of the slice: x: 2, y: 2, z: 4, core: 2. Of those that a mesh axis runs over, the one named last changes fastest.
Arguments:
- queries: bfloat16 [2048, 3072], P(('parts', 'ctx', 'pb', 'row')), may hold values from -10 to 10
- cache_keys: bfloat16 [4096, 192], P(('parts', 'ctx')), may hold values from -10 to 10
- cache_values: bfloat16 [4096, 128], P(('parts', 'ctx')), may hold values from -6 to 6
- span_keys: bfloat16 [2048, 192], P(('parts', 'ctx')), may hold values from -10 to 10
- span_values: bfloat16 [2048, 128], P(('parts', 'ctx')), may hold values from -6 to 6
- pool_keys: float32 [32, 192], replicated, may hold values from 0.2 to 0.6
- pool_values: float32 [32, 128], replicated, may hold values from 0.05 to 0.3
- gate_logits: bfloat16 [2048, 48], P(('parts', 'ctx', 'pb', 'row')), may hold values from -6 to 6
- chosen_blocks: int32 [32, 16], P(('parts', 'ctx', 'pb', 'row')), may hold values from 0 to 95, as said below
- valid_counts: int32 [32], P(('parts', 'ctx', 'pb', 'row')), may hold values from 4 to 16
Outputs:
- mixed: bfloat16 [2048, 2048], P(('parts', 'ctx', 'pb', 'row'))
Inputs may be any that keep to these rules, and one draw needn't show every extreme that they name: `chosen_blocks`: slot 0 of tile t holds the tile's own block 64 + t. Slot s > 0 holds a block of the cache stored by ctx index (c + s) mod (4), where c is the ctx index that holds tile t; the blocks of one tile are distinct. Slots at or beyond the tile's valid count hold blocks too and are ignored.
All inputs are finite; a program needn't handle non-finite values.
Results may differ from a plain program's by a relative error of at most 0.0034.
The roundings to bfloat16 on the way count: a program that leaves them out, or rounds other values in their place, can miss the bound.
Values may be sent and summed in bfloat16 or wider, within the bound.
A program may use at most 64 MiB of HBM per device.

v0:
```python
import math
import jax
import jax.numpy as jnp
from jax import lax
from jax.sharding import PartitionSpec as P

HEADS = 16
CLEN = 32
STRIDE = 16
BLOCK = 64
WINDOW = 256
NEG_FILL = -1e30


def from_behind(value, axis, steps):
    count = lax.axis_size(axis)
    pairs = [(source, (source + steps) % count) for source in range(count)]
    return lax.ppermute(value, axis, pairs)


def pool_blocks(rows, extra, weights, stride):
    joined = jnp.concatenate([rows, extra], axis=0).astype(jnp.float32)
    blocks = rows.shape[0] // stride
    grouped = joined.reshape(blocks + 1, stride, rows.shape[1])
    leading = jnp.sum(grouped[:-1] * weights[None, :stride, :], axis=1)
    trailing = jnp.sum(grouped[1:] * weights[None, stride:, :], axis=1)
    return (leading + trailing).astype(jnp.bfloat16)


def attend(query_rows, keys, values, visible, score_scale):
    scores = jnp.dot(query_rows, keys.T, preferred_element_type=jnp.float32) * score_scale
    scores = jnp.where(visible, scores, NEG_FILL)
    highest = jnp.max(scores, axis=1, keepdims=True)
    exponent = jnp.where(visible, jnp.exp(scores - highest), 0.0)
    weights = exponent.astype(jnp.bfloat16)
    numerator = jnp.dot(weights, values, preferred_element_type=jnp.float32)
    return numerator / jnp.sum(exponent, axis=1, keepdims=True)


def local(
    queries,
    cache_keys,
    cache_values,
    span_keys,
    span_values,
    pool_keys,
    pool_values,
    gate_logits,
    chosen_blocks,
    valid_counts,
):
    owners = lax.axis_size("ctx")
    ctx_place = lax.axis_index("ctx")
    tile_place = lax.axis_index("pb") * lax.axis_size("row") + lax.axis_index("row")
    cache_len, key_width = cache_keys.shape
    value_width = cache_values.shape[1]
    span_len = span_keys.shape[0]
    tokens = queries.shape[0]
    tiles_here = chosen_blocks.shape[0]
    score_scale = 1.0 / math.sqrt(key_width)
    context_start = cache_len * owners
    local_start = tile_place * tokens
    first_pos = context_start + ctx_place * span_len + local_start
    row_count = tokens * HEADS
    query_rows = queries.reshape(row_count, key_width)
    row_pos = first_pos + jnp.arange(row_count, dtype=jnp.int32) // HEADS
    leader = ctx_place == 0
    outgoing = (
        jnp.where(leader, span_keys[:STRIDE], cache_keys[:STRIDE]),
        jnp.where(leader, span_values[:STRIDE], cache_values[:STRIDE]),
        span_keys[:STRIDE],
        span_values[:STRIDE],
    )
    heads_next = from_behind((outgoing[0], outgoing[1], outgoing[2], outgoing[3]), "ctx", -1)
    summary_keys = jnp.concatenate(
        [
            pool_blocks(cache_keys, heads_next[0], pool_keys, STRIDE),
            pool_blocks(span_keys, heads_next[2], pool_keys, STRIDE),
        ],
        axis=0,
    )
    summary_values = jnp.concatenate(
        [
            pool_blocks(cache_values, heads_next[1], pool_values, STRIDE),
            pool_blocks(span_values, heads_next[3], pool_values, STRIDE),
        ],
        axis=0,
    )
    cache_blocks = cache_len // STRIDE
    span_blocks = span_len // STRIDE
    per_ctx = cache_blocks + span_blocks
    first_row = jnp.int32(0)
    running_max = jnp.full((row_count,), NEG_FILL, jnp.float32)
    running_sum = jnp.zeros((row_count,), jnp.float32)
    running_out = jnp.zeros((row_count, value_width), jnp.float32)
    part_keys = lax.all_gather(summary_keys, "ctx", axis=0, tiled=True)
    part_values = lax.all_gather(summary_values, "ctx", axis=0, tiled=True)
    length = part_keys.shape[0]
    for lower_row in range(0, length, 512):
        upper_row = min(lower_row + 512, length)
        block_index = first_row + lower_row + jnp.arange(upper_row - lower_row, dtype=jnp.int32)
        owner_of = block_index // per_ctx
        within = block_index % per_ctx
        block_id = jnp.where(
            within < cache_blocks,
            owner_of * cache_blocks + within,
            owners * cache_blocks + owner_of * span_blocks + within - cache_blocks,
        )
        visible = (block_id * STRIDE + CLEN)[None, :] <= row_pos[:, None] + 1
        scores = (
            jnp.dot(
                query_rows, part_keys[lower_row:upper_row].T, preferred_element_type=jnp.float32
            )
            * score_scale
        )
        scores = jnp.where(visible, scores, NEG_FILL)
        new_max = jnp.maximum(running_max, jnp.max(scores, axis=1))
        exponent = jnp.where(visible, jnp.exp(scores - new_max[:, None]), 0.0)
        fading = jnp.exp(running_max - new_max)
        running_sum = running_sum * fading + jnp.sum(exponent, axis=1)
        running_out = running_out * fading[:, None] + jnp.dot(
            exponent.astype(jnp.bfloat16),
            part_values[lower_row:upper_row],
            preferred_element_type=jnp.float32,
        )
        running_max = new_max
    summary_out = running_out / running_sum[:, None]
    reach = chosen_blocks.shape[1] // owners
    arranged = chosen_blocks.reshape(tiles_here, reach, owners)
    column_of = (jnp.arange(owners, dtype=jnp.int32) - ctx_place) % owners
    requested = jnp.take(arranged, column_of, axis=2)
    wanted = lax.all_to_all(requested, "ctx", split_axis=2, concat_axis=2, tiled=True)
    cache_count = cache_len // BLOCK
    span_count = span_len // BLOCK
    from_cache = (wanted < owners * cache_count)[..., None, None]
    cache_slot = jnp.clip(wanted - ctx_place * cache_count, 0, cache_count - 1)
    span_slot = jnp.clip(wanted - owners * cache_count - ctx_place * span_count, 0, span_count - 1)
    served_keys = jnp.where(
        from_cache,
        cache_keys.reshape(cache_count, BLOCK, key_width)[cache_slot],
        span_keys.reshape(span_count, BLOCK, key_width)[span_slot],
    )
    served_values = jnp.where(
        from_cache,
        cache_values.reshape(cache_count, BLOCK, value_width)[cache_slot],
        span_values.reshape(span_count, BLOCK, value_width)[span_slot],
    )
    fetched_keys, fetched_values = (
        lax.all_to_all(served_keys, "ctx", split_axis=2, concat_axis=2, tiled=True),
        lax.all_to_all(served_values, "ctx", split_axis=2, concat_axis=2, tiled=True),
    )
    last_ctx = ctx_place == owners - 1
    tail_rows = from_behind(
        (
            jnp.where(last_ctx, cache_keys[-WINDOW:], span_keys[-WINDOW:]),
            jnp.where(last_ctx, cache_values[-WINDOW:], span_values[-WINDOW:]),
        ),
        "ctx",
        1,
    )
    reach_keys = jnp.concatenate([tail_rows[0], span_keys], axis=0)
    reach_values = jnp.concatenate([tail_rows[1], span_values], axis=0)
    gate_values = jax.nn.sigmoid(gate_logits.astype(jnp.float32)).reshape(tokens, 3, HEADS)
    offsets = jnp.arange(BLOCK, dtype=jnp.int32)
    near_offsets = jnp.arange(WINDOW + BLOCK, dtype=jnp.int32)
    slot_number = jnp.arange(reach, dtype=jnp.int32)[:, None] * owners + column_of[None, :]
    key_pos = (requested[0][:, :, None] * BLOCK + offsets).reshape(-1)
    usable = jnp.repeat((slot_number < valid_counts[0]).reshape(-1), BLOCK)
    sel_visible = usable[None, :] & (key_pos[None, :] <= row_pos[:, None])
    picked = attend(
        query_rows,
        fetched_keys[0].reshape(-1, key_width),
        fetched_values[0].reshape(-1, value_width),
        sel_visible,
        score_scale,
    )
    begin = local_start + 0
    near_keys = lax.dynamic_slice_in_dim(reach_keys, begin, WINDOW + BLOCK, 0)
    near_values = lax.dynamic_slice_in_dim(reach_values, begin, WINDOW + BLOCK, 0)
    near_pos = context_start + ctx_place * span_len - WINDOW + begin + near_offsets
    near_visible = (near_pos[None, :] <= row_pos[:, None]) & (
        near_pos[None, :] > row_pos[:, None] - WINDOW
    )
    nearby = attend(query_rows, near_keys, near_values, near_visible, score_scale)
    mixed = (
        gate_values[:, 0, :, None] * summary_out.reshape(BLOCK, HEADS, value_width)
        + gate_values[:, 1, :, None] * picked.reshape(BLOCK, HEADS, value_width)
        + gate_values[:, 2, :, None] * nearby.reshape(BLOCK, HEADS, value_width)
    )
    outputs = mixed.reshape(BLOCK, HEADS * value_width).astype(jnp.bfloat16)
    return outputs


def solution(mesh):
    return jax.shard_map(
        local,
        mesh=mesh,
        in_specs=(
            P(("parts", "ctx", "pb", "row"), None),
            P(("parts", "ctx"), None),
            P(("parts", "ctx"), None),
            P(("parts", "ctx"), None),
            P(("parts", "ctx"), None),
            P(),
            P(),
            P(("parts", "ctx", "pb", "row"), None),
            P(("parts", "ctx", "pb", "row"), None),
            P(("parts", "ctx", "pb", "row")),
        ),
        out_specs=P(("parts", "ctx", "pb", "row"), None),
        check_vma=False,
    )
```

profile of v0, /device:TPU:0, one launch (start us, length us, event | category | flops | bytes accessed | tf_op | source)
XLA Modules:
  0.0 91.8 jit_solution(5316688061465802636)
XLA Ops:
  0.0 1.3 %copy.79 = bf16[1024,192]{1,0:T(8,128)(2,1)S(1)} copy(bf16[1024,192]{0,1:T(8,128)(2,1)} %param.11) | data formatting | bytes 786432 | tf_op args[1]
  1.3 1.1 %copy.77 = bf16[512,192]{1,0:T(8,128)(2,1)S(1)} copy(bf16[512,192]{0,1:T(8,128)(2,1)} %param.13) | data formatting | bytes 393216 | tf_op args[3]
  3.0 5.1 %collective-permute-start = (bf16[16,192]{1,0:T(8,128)(2,1)}, bf16[16,192]{1,0:T(8,128)(2,1)}, u32[]{:S(2)}, u32[]{:S(2)}) collective-permute-start(bf16[16,192]{1,0:T(8,128)(2,1)} %get-tuple-element.13), channel_id=1, source_target_pairs={{0,24},{8,0},{16,8},{24,16},{1,25},{9,1},{17,9},{25,17},{2,26},{10... | collective-permute-start | bytes 18440 | tf_op jit(solution)/shard_map/ppermute | solution.py:18
  8.5 1.3 %slice_select_fusion.3 = (bf16[16,128]{1,0:T(8,128)(2,1)}, bf16[16,128]{1,0:T(8,128)(2,1)}) fusion(bf16[1024,128]{1,0:T(8,128)(2,1)} %param.12, pred[]{:T(512)S(6)} %eq.10, bf16[512,128]{1,0:T(8,128)(2,1)} %param.14), kind=kLoop, calls=%fused_computation.87 | loop fusion | flops 2048 | bytes 16385 | tf_op jit(solution)/shard_map/jit(_where)/select_n | solution.py:70
  10.8 1.3 %reduce.3 = s32[16]{0:T(128)S(1)} reduce(s32[1,16]{1,0:T(1,128)} %param.18, s32[]{:T(128)} %broadcast.494), dimensions={0}, to_apply=%param.18.reduce_sub_computation.3 | reduce | bytes 132 | tf_op args[8]
  13.0 0.7 copy.85
  13.7 5.3 %all-to-all-start = ((s32[1,4,4]{1,0,2:T(1,128)}), s32[1,4,4]{1,0,2:T(1,128)S(1)}, u32[]{:S(2)}, u32[]{:S(2)}) async-start(s32[1,4,4]{1,0,2:T(1,128)} %copy.85), calls=%async_computation | async-start | bytes 4096 | tf_op jit(solution)/shard_map/all_to_all | solution.py:132
  18.9 1.0 %slice_select_fusion = bf16[256,192]{0,1:T(8,128)(2,1)S(1)} fusion(bf16[512,192]{0,1:T(8,128)(2,1)} %param.13, bf16[1024,192]{0,1:T(8,128)(2,1)} %param.11, pred[]{:T(512)S(6)} %eq.11), kind=kLoop, calls=%fused_computation.60 | loop fusion | flops 49152 | bytes 294913 | tf_op jit(solution)/shard_map/jit(_where)/select_n | solution.py:155
  19.9 2.1 %collective-permute-start.4 = (bf16[256,192]{0,1:T(8,128)(2,1)S(1)}, bf16[256,192]{0,1:T(8,128)(2,1)}, u32[]{:S(2)}, u32[]{:S(2)}) collective-permute-start(bf16[256,192]{0,1:T(8,128)(2,1)S(1)} %slice_select_fusion), channel_id=1, source_target_pairs={{0,8},{8,16},{16,24},{24,0},{1,9},{9,17},{17,25},{25,1},{2,10},{10... | collective-permute-start | bytes 294920 | tf_op jit(solution)/shard_map/ppermute | solution.py:18
  24.5 0.6 and.99
  25.2 0.7 copy.76
  25.9 0.7 copy.81
  26.6 0.7 copy.97
  30.3 0.7 copy.95
  31.1 3.6 %all-to-all-start.2 = ((bf16[1,4,4,64,128]{4,3,1,0,2:T(8,128)(2,1)}), bf16[1,4,4,64,128]{4,3,1,0,2:T(8,128)(2,1)S(1)}, u32[]{:S(2)}, u32[]{:S(2)}) async-start(bf16[1,4,4,64,128]{4,3,1,0,2:T(8,128)(2,1)} %copy.95), calls=%async_computation.2 | async-start | bytes 524288 | tf_op jit(solution)/shard_map/all_to_all | solution.py:150
  34.7 0.9 copy_select_fusion
  35.6 2.0 %collective-permute-start.5 = (bf16[256,128]{1,0:T(8,128)(2,1)S(1)}, bf16[256,128]{1,0:T(8,128)(2,1)}, u32[]{:S(2)}, u32[]{:S(2)}) collective-permute-start(bf16[256,128]{1,0:T(8,128)(2,1)S(1)} %slice_select_fusion.1), channel_id=1, source_target_pairs={{0,8},{8,16},{16,24},{24,0},{1,9},{9,17},{17,25},{25,1},{2,10},{10... | collective-permute-start | bytes 196616 | tf_op jit(solution)/shard_map/ppermute | solution.py:18
  37.6 0.7 maximum_convert_fusion.2
  38.4 0.7 maximum_convert_fusion.3
  39.6 13.2 %all_gather.7 = bf16[384,128]{1,0:T(8,128)(2,1)S(1)} all-gather(bf16[96,128]{1,0:T(8,128)(2,1)S(1)} %pad_maximum_fusion.1), channel_id=1, replica_groups=mesh['parts'=1,'ctx'=4,'pb'=4,'row'=2] {'ctx'}, dimensions={0}, use_global_device_ids=true | all-gather | bytes 122880 | tf_op jit(solution)/shard_map/all_gather | solution.py:97
  52.8 0.8 maximum_convert_fusion
  53.8 0.7 maximum_convert_fusion.1
  55.5 13.6 %all_gather.6 = bf16[384,192]{1,0:T(8,128)(2,1)S(1)} all-gather(bf16[96,192]{1,0:T(8,128)(2,1)S(1)} %pad_maximum_fusion), channel_id=1, replica_groups=mesh['parts'=1,'ctx'=4,'pb'=4,'row'=2] {'ctx'}, dimensions={0}, use_global_device_ids=true | all-gather | bytes 184320 | tf_op jit(solution)/shard_map/all_gather | solution.py:96
  69.8 0.7 fusion.5
  70.6 3.7 %all-to-all-start.1 = ((bf16[1,4,4,64,192]{4,3,1,0,2:T(8,128)(2,1)}), bf16[1,4,4,64,192]{4,3,1,0,2:T(8,128)(2,1)S(1)}, u32[]{:S(2)}, u32[]{:S(2)}) async-start(bf16[1,4,4,64,192]{4,3,1,0,2:T(8,128)(2,1)} %copy_select_fusion), calls=%async_computation.1 | async-start | bytes 1048576 | tf_op jit(solution)/shard_map/all_to_all | solution.py:149
  74.3 1.7 %fusion.59 = (f32[1024]{0:T(1024)S(1)}, f32[1024,320]{0,1:T(8,128)S(1)}) fusion(bf16[1024,192]{1,0:T(8,128)(2,1)S(1)} %reshape.297, s32[]{:T(128)S(6)} %select_n.211, bf16[256,192]{0,1:T(8,128)(2,1)} %collective-permute-done.4, bf16[512,192]{0,1:T(8,128)(2,1)S(1)} %copy-done.2, s32[1024]{0:T(1024)S(1)} %broadcast_add_fusion, s32[1024]{0:T(1024)S(1)} %fusion.31, ...), kind=kOutput, calls=%fused_computation.137 | convolution fusion | flops 128039936 | bytes 2012420 | tf_op jit(solution)/shard_map/dot_general | solution.py:31
  76.4 1.5 %convolution_divide_fusion = f32[1024,128]{1,0:T(8,128)S(1)} fusion(f32[1024,320]{0,1:T(8,128)S(1)} %get-tuple-element.29, f32[1024]{0:T(1024)S(1)} %get-tuple-element.28, s32[1024]{0:T(1024)S(1)} %broadcast_add_fusion, s32[1024]{0:T(1024)S(1)} %fusion.31, s32[320]{0:T(512)S(1)} %iota_add_fusion.1, f32[1024]{0:T(1024)S(1)} %fusion.11, s32[]{:T(128)S(6)} %select_n.211, ...), kind=kOutput, calls=%fused_computation.21 | convolution fusion | flops 86147072 | bytes 2049284 | tf_op jit(solution)/shard_map/dot_general | solution.py:36
  78.0 6.4 %all-to-all-done.1 = bf16[1,4,4,64,192]{4,3,1,0,2:T(8,128)(2,1)S(1)} async-done(((bf16[1,4,4,64,192]{4,3,1,0,2:T(8,128)(2,1)}), bf16[1,4,4,64,192]{4,3,1,0,2:T(8,128)(2,1)S(1)}, u32[]{:S(2)}, u32[]{:S(2)}) %all-to-all-start.1) | async-done | bytes 393248 | tf_op jit(solution)/shard_map/all_to_all | solution.py:149
  84.4 1.2 %fusion = (f32[1024]{0:T(1024)S(1)}, f32[1024,1024]{1,0:T(8,128)S(1)}) fusion(s32[1024]{0:T(1024)S(1)} %fusion.31, s32[1024]{0:T(1024)S(1)} %add.265, pred[1024]{0:T(1024)(128)(4,1)S(1)} %copy-done.11, bf16[1024,192]{1,0:T(8,128)(2,1)S(1)} %bitcast.97, bf16[1024,192]{1,0:T(8,128)(2,1)S(1)} %reshape.297), kind=kOutput, calls=%fused_computation.8 | convolution fusion | flops 407895040 | bytes 4994048 | tf_op jit(solution)/shard_map/dot_general | solution.py:31
  85.6 1.9 %fusion.52 = f32[1024]{0:T(1024)S(1)} fusion(f32[1024]{0:T(1024)S(1)} %get-tuple-element.30, f32[1024,1024]{1,0:T(8,128)S(1)} %get-tuple-element.31, s32[1024]{0:T(1024)S(1)} %fusion.31, s32[1024]{0:T(1024)S(1)} %add.265, pred[1024]{0:T(1024)(128)(4,1)S(1)} %copy-done.11), kind=kLoop, calls=%fused_computation.130 | loop fusion | flops 7339008 | bytes 4211712 | tf_op jit(solution)/shard_map/reduce_sum | solution.py:37
  87.5 1.8 %fusion.6 = f32[1024,128]{1,0:T(8,128)S(1)} fusion(bf16[1024,128]{1,0:T(8,128)(2,1)S(1)} %bitcast.98, f32[1024]{0:T(1024)S(1)} %fusion.52, f32[1024,1024]{1,0:T(8,128)S(1)} %get-tuple-element.31, f32[1024]{0:T(1024)S(1)} %get-tuple-element.30, s32[1024]{0:T(1024)S(1)} %fusion.31, s32[1024]{0:T(1024)S(1)} %add.265, pred[1024]{0:T(1024)(128)(4,1)S(1)} %copy-done.11), kind=kOutput, calls=%fused_computation.20 | convolution fusion | flops 275906560 | bytes 4998144 | tf_op jit(solution)/shard_map/dot_general | solution.py:36
  90.6 1.3 %fusion.25 = bf16[64,2048]{1,0:T(8,128)(2,1)} fusion(f32[64,2048]{1,0:T(8,128)S(1)} %reshape.305, f32[8,8,16,128]{3,2,1,0:T(8,128)S(1)} %bitcast.92, f32[64,2048]{1,0:T(8,128)S(1)} %reshape.304, f32[8,8,16,128]{3,2,1,0:T(8,128)S(1)} %bitcast.91, f32[64,2048]{1,0:T(8,128)S(1)} %reshape.298, f32[8,8,16,128]{3,2,1,0:T(8,128)S(1)} %bitcast.90), kind=kLoop, calls=%fused_computation.40 | loop fusion | flops 786432 | bytes 3407872 | tf_op jit(solution)/shard_map/convert_element_type | solution.py:190
  (107 shorter events, 11.9 us)
Async XLA Ops:
  0.0 22.7 %copy-start.1 = (bf16[1024,128]{1,0:T(8,128)(2,1)S(1)}, bf16[1024,128]{1,0:T(8,128)(2,1)}, u32[]{:S(2)}) copy-start(bf16[1024,128]{1,0:T(8,128)(2,1)} %param.12) | copy-start | bytes 786436
  0.0 22.7 %copy-start = (bf16[512,128]{1,0:T(8,128)(2,1)S(1)}, bf16[512,128]{1,0:T(8,128)(2,1)}, u32[]{:S(2)}) copy-start(bf16[512,128]{1,0:T(8,128)(2,1)} %param.14) | copy-start | bytes 393220
  0.0 22.7 %copy-start.7 = (f32[32,192]{1,0:T(8,128)S(1)}, f32[32,192]{1,0:T(8,128)}, u32[]{:S(2)}) copy-start(f32[32,192]{1,0:T(8,128)} %param.15) | copy-start | bytes 73732
  0.0 22.7 %copy-start.3 = (bf16[64,3072]{1,0:T(8,128)(2,1)S(1)}, bf16[64,3072]{1,0:T(8,128)(2,1)}, u32[]{:S(2)}) copy-start(bf16[64,3072]{1,0:T(8,128)(2,1)} %param.10) | copy-start | bytes 1179652
  0.0 23.4 %copy-start.8 = (f32[32,128]{1,0:T(8,128)S(1)}, f32[32,128]{1,0:T(8,128)}, u32[]{:S(2)}) copy-start(f32[32,128]{1,0:T(8,128)} %param.16) | copy-start | bytes 49156
  0.0 25.2 %copy-start.9 = (bf16[64,48]{0,1:T(8,128)(2,1)S(1)}, bf16[64,48]{0,1:T(8,128)(2,1)}, u32[]{:S(2)}) copy-start(bf16[64,48]{0,1:T(8,128)(2,1)} %param.17) | copy-start | bytes 18436
  3.0 49.8 %collective-permute-start = (bf16[16,192]{1,0:T(8,128)(2,1)}, bf16[16,192]{1,0:T(8,128)(2,1)}, u32[]{:S(2)}, u32[]{:S(2)}) collective-permute-start(bf16[16,192]{1,0:T(8,128)(2,1)} %get-tuple-element.13), channel_id=1, source_target_pairs={{0,24},{8,0},{16,8},{24,16},{1,25},{9,1},{17,9},{25,17},{2,26},{10... | collective-permute-start | bytes 18440 | tf_op jit(solution)/shard_map/ppermute | solution.py:18
  8.0 45.7 %collective-permute-start.1 = (bf16[16,192]{1,0:T(8,128)(2,1)}, bf16[16,192]{1,0:T(8,128)(2,1)}, u32[]{:S(2)}, u32[]{:S(2)}) collective-permute-start(bf16[16,192]{1,0:T(8,128)(2,1)} %get-tuple-element.14), channel_id=1, source_target_pairs={{0,24},{8,0},{16,8},{24,16},{1,25},{9,1},{17,9},{25,17},{2,26},{10... | collective-permute-start | bytes 18440 | tf_op jit(solution)/shard_map/ppermute | solution.py:18
  9.8 25.8 %collective-permute-start.2 = (bf16[16,128]{1,0:T(8,128)(2,1)}, bf16[16,128]{1,0:T(8,128)(2,1)}, u32[]{:S(2)}, u32[]{:S(2)}) collective-permute-start(bf16[16,128]{1,0:T(8,128)(2,1)} %get-tuple-element.15), channel_id=1, source_target_pairs={{0,24},{8,0},{16,8},{24,16},{1,25},{9,1},{17,9},{25,17},{2,26},{10... | collective-permute-start | bytes 12296 | tf_op jit(solution)/shard_map/ppermute | solution.py:18
  10.2 28.2 %collective-permute-start.3 = (bf16[16,128]{1,0:T(8,128)(2,1)}, bf16[16,128]{1,0:T(8,128)(2,1)}, u32[]{:S(2)}, u32[]{:S(2)}) collective-permute-start(bf16[16,128]{1,0:T(8,128)(2,1)} %get-tuple-element.16), channel_id=1, source_target_pairs={{0,24},{8,0},{16,8},{24,16},{1,25},{9,1},{17,9},{25,17},{2,26},{10... | collective-permute-start | bytes 12296 | tf_op jit(solution)/shard_map/ppermute | solution.py:18
  13.7 13.6 %all-to-all-start = ((s32[1,4,4]{1,0,2:T(1,128)}), s32[1,4,4]{1,0,2:T(1,128)S(1)}, u32[]{:S(2)}, u32[]{:S(2)}) async-start(s32[1,4,4]{1,0,2:T(1,128)} %copy.85), calls=%async_computation | async-start | bytes 4096 | tf_op jit(solution)/shard_map/all_to_all | solution.py:132
  19.9 54.4 %collective-permute-start.4 = (bf16[256,192]{0,1:T(8,128)(2,1)S(1)}, bf16[256,192]{0,1:T(8,128)(2,1)}, u32[]{:S(2)}, u32[]{:S(2)}) collective-permute-start(bf16[256,192]{0,1:T(8,128)(2,1)S(1)} %slice_select_fusion), channel_id=1, source_target_pairs={{0,8},{8,16},{16,24},{24,0},{1,9},{9,17},{17,25},{25,1},{2,10},{10... | collective-permute-start | bytes 294920 | tf_op jit(solution)/shard_map/ppermute | solution.py:18
  31.1 39.6 %all-to-all-start.2 = ((bf16[1,4,4,64,128]{4,3,1,0,2:T(8,128)(2,1)}), bf16[1,4,4,64,128]{4,3,1,0,2:T(8,128)(2,1)S(1)}, u32[]{:S(2)}, u32[]{:S(2)}) async-start(bf16[1,4,4,64,128]{4,3,1,0,2:T(8,128)(2,1)} %copy.95), calls=%async_computation.2 | async-start | bytes 524288 | tf_op jit(solution)/shard_map/all_to_all | solution.py:150
  35.6 40.8 %collective-permute-start.5 = (bf16[256,128]{1,0:T(8,128)(2,1)S(1)}, bf16[256,128]{1,0:T(8,128)(2,1)}, u32[]{:S(2)}, u32[]{:S(2)}) collective-permute-start(bf16[256,128]{1,0:T(8,128)(2,1)S(1)} %slice_select_fusion.1), channel_id=1, source_target_pairs={{0,8},{8,16},{16,24},{24,0},{1,9},{9,17},{17,25},{25,1},{2,10},{10... | collective-permute-start | bytes 196616 | tf_op jit(solution)/shard_map/ppermute | solution.py:18
  54.6 14.4 %copy-start.10 = (s32[384]{0:T(512)S(1)}, s32[384]{0:T(512)}, u32[]{:S(2)}) copy-start(s32[384]{0:T(512)} %multiply_add_fusion) | copy-start | bytes 4612
  70.5 3.8 %copy-start.2 = (bf16[512,192]{0,1:T(8,128)(2,1)S(1)}, bf16[512,192]{0,1:T(8,128)(2,1)}, u32[]{:S(2)}) copy-start(bf16[512,192]{0,1:T(8,128)(2,1)} %param.13) | copy-start | bytes 589828
  70.6 13.7 %all-to-all-start.1 = ((bf16[1,4,4,64,192]{4,3,1,0,2:T(8,128)(2,1)}), bf16[1,4,4,64,192]{4,3,1,0,2:T(8,128)(2,1)S(1)}, u32[]{:S(2)}, u32[]{:S(2)}) async-start(bf16[1,4,4,64,192]{4,3,1,0,2:T(8,128)(2,1)} %copy_select_fusion), calls=%async_computation.1 | async-start | bytes 1048576 | tf_op jit(solution)/shard_map/all_to_all | solution.py:149
  77.9 6.5 %copy-start.11 = (pred[1024]{0:T(1024)(128)(4,1)S(1)}, pred[1024]{0:T(1024)(128)(4,1)}, u32[]{:S(2)}) copy-start(pred[1024]{0:T(1024)(128)(4,1)} %and.99) | copy-start | bytes 3076
  87.5 2.0 %copy-start.4 = (f32[64,16]{1,0:T(8,128)S(1)}, f32[64,16]{1,0:T(8,128)}, u32[]{:S(2)}) copy-start(f32[64,16]{1,0:T(8,128)} %copy.76) | copy-start | bytes 12292
  89.4 0.8 copy-start.5
  89.4 0.9 %copy-start.6 = (f32[64,16]{1,0:T(8,128)S(1)}, f32[64,16]{1,0:T(8,128)}, u32[]{:S(2)}) copy-start(f32[64,16]{1,0:T(8,128)} %copy.97) | copy-start | bytes 12292
where the time goes:
time: 92.6 us; the launch traced here: 91.8 us
  blocking collectives  26.8 us (29%)
  starting transfers between devices  22.7 us (25%)
  other arithmetic  14.1 us (15%)
  local copies, waits for them, and re-layouts  13.3 us (14%)
  matrix products  7.31 us (8%)
  waiting for transfers between devices  6.38 us (7%)
  between operations  1.25 us (1%)
    all_gather x1, blocking collectives, local(): part_keys = lax.all_gather(summary_keys, 'ctx', axis=0, tiled=True)  13.6 us
    all_gather x1, blocking collectives, local(): part_values = lax.all_gather(summary_values, 'ctx', axis=0, tiled=True)  13.2 us
    ppermute x6, starting transfers between devices, from_behind(): return lax.ppermute(value, axis, pairs)  10.1 us
    all_to_all x1, waiting for transfers between devices, local(): lax.all_to_all(served_keys, 'ctx', split_axis=2, concat_axis=2, tiled=True)  6.36 us
    all_to_all x1, starting transfers between devices, local(): lax.all_to_all(requested, 'ctx', split_axis=2, concat_axis=2, tiled=True)  5.27 us
    all_to_all x1, starting transfers between devices, local(): lax.all_to_all(served_keys, 'ctx', split_axis=2, concat_axis=2, tiled=True)  3.66 us
    all_to_all x1, starting transfers between devices, local(): lax.all_to_all(served_values, 'ctx', split_axis=2, concat_axis=2, tiled=T...  3.63 us
    unnamed x27, local copies, waits for them, and re-layouts  3.33 us
  transfers between devices with their start and end apart: 9, of which 1 were waited for; matrix products, arithmetic and copies ran while one was open for 27% of the time, Pallas kernels for 0%

commit v1 on v0

--- a/solution.py
+++ b/solution.py
@@ -10,6 +10,12 @@
 BLOCK = 64
 WINDOW = 256
 NEG_FILL = -1e30
+
+
+def trade_parts(block, name, split, join):
+    parts = jnp.split(block, lax.axis_size(name), axis=split)
+    received = lax.all_to_all(jnp.stack(parts), name, 0, 0)
+    return jnp.concatenate(received, axis=join)
 
 
 def from_behind(value, axis, steps):
@@ -129,7 +135,7 @@
     arranged = chosen_blocks.reshape(tiles_here, reach, owners)
     column_of = (jnp.arange(owners, dtype=jnp.int32) - ctx_place) % owners
     requested = jnp.take(arranged, column_of, axis=2)
-    wanted = lax.all_to_all(requested, "ctx", split_axis=2, concat_axis=2, tiled=True)
+    wanted = trade_parts(requested, "ctx", 2, 2)
     cache_count = cache_len // BLOCK
     span_count = span_len // BLOCK
     from_cache = (wanted < owners * cache_count)[..., None, None]

time: 92.6 us -> 98.8 us (1.067)
  other arithmetic: 14.1 us -> 19.6 us
    lt x0 -> x2, local copies, waits for them, and re-layouts: none -> 1.27 us  [local(): from_cache = (wanted < owners * cache_count)[..., None, None]]
    unnamed x27 -> x39, local copies, waits for them, and re-layouts: 3.33 us -> 3.38 us
  transfers between devices with their start and end apart: 9 -> 9, of which waited for: 1 -> 1; matrix products, arithmetic and copies ran while one was open for 27% -> 30% of each run, Pallas kernels for 0% -> 0%
where the time goes in v1:
time: 98.8 us; the launch traced here: 98 us
  blocking collectives  26.8 us (27%)
  starting transfers between devices  22.6 us (23%)
  other arithmetic  19.6 us (20%)
  local copies, waits for them, and re-layouts  14.1 us (14%)
  waiting for transfers between devices  7.18 us (7%)
  matrix products  6.48 us (7%)
  between operations  1.27 us (1%)
    all_gather x1, blocking collectives, local(): part_keys = lax.all_gather(summary_keys, 'ctx', axis=0, tiled=True)  13.6 us
    all_gather x1, blocking collectives, local(): part_values = lax.all_gather(summary_values, 'ctx', axis=0, tiled=True)  13.2 us
    ppermute x6, starting transfers between devices, from_behind(): return lax.ppermute(value, axis, pairs)  10.1 us
    all_to_all x1, waiting for transfers between devices, local(): lax.all_to_all(served_keys, 'ctx', split_axis=2, concat_axis=2, tiled=True)  7.16 us
    all_to_all x1, starting transfers between devices, trade_parts(): received = lax.all_to_all(jnp.stack(parts), name, 0, 0)  5.27 us
    all_to_all x1, starting transfers between devices, local(): lax.all_to_all(served_keys, 'ctx', split_axis=2, concat_axis=2, tiled=True)  3.66 us
    all_to_all x1, starting transfers between devices, local(): lax.all_to_all(served_values, 'ctx', split_axis=2, concat_axis=2, tiled=T...  3.63 us
    unnamed x39, local copies, waits for them, and re-layouts  3.38 us
  transfers between devices with their start and end apart: 9, of which 1 were waited for; matrix products, arithmetic and copies ran while one was open for 30% of the time, Pallas kernels for 0%

profile of v1, /device:TPU:0, one launch (start us, length us, event | category | flops | bytes accessed | tf_op | source)
XLA Modules:
  0.0 98.0 jit_solution(7257098998032914413)
XLA Ops:
  0.0 1.3 %copy.62 = bf16[1024,192]{1,0:T(8,128)(2,1)S(1)} copy(bf16[1024,192]{0,1:T(8,128)(2,1)} %param.11) | data formatting | bytes 786432 | tf_op args[1]
  1.3 1.1 %copy.60 = bf16[512,192]{1,0:T(8,128)(2,1)S(1)} copy(bf16[512,192]{0,1:T(8,128)(2,1)} %param.13) | data formatting | bytes 393216 | tf_op args[3]
  3.0 5.1 %collective-permute-start = (bf16[16,192]{1,0:T(8,128)(2,1)}, bf16[16,192]{1,0:T(8,128)(2,1)}, u32[]{:S(2)}, u32[]{:S(2)}) collective-permute-start(bf16[16,192]{1,0:T(8,128)(2,1)} %get-tuple-element.17), channel_id=1, source_target_pairs={{0,24},{8,0},{16,8},{24,16},{1,25},{9,1},{17,9},{25,17},{2,26},{10... | collective-permute-start | bytes 18440 | tf_op jit(solution)/shard_map/ppermute | solution.py:24
  8.5 1.3 %slice_select_fusion.3 = (bf16[16,128]{1,0:T(8,128)(2,1)}, bf16[16,128]{1,0:T(8,128)(2,1)}) fusion(bf16[1024,128]{1,0:T(8,128)(2,1)} %param.12, pred[]{:T(512)S(6)} %eq.10, bf16[512,128]{1,0:T(8,128)(2,1)} %param.14), kind=kLoop, calls=%fused_computation.88 | loop fusion | flops 2048 | bytes 16385 | tf_op jit(solution)/shard_map/jit(_where)/select_n | solution.py:76
  10.9 1.3 %reduce.11 = s32[16]{0:T(128)S(1)} reduce(s32[1,16]{1,0:T(1,128)} %param.18, s32[]{:T(128)} %broadcast.555), dimensions={0}, to_apply=%param.18.reduce_sub_computation.3 | reduce | bytes 132 | tf_op args[8]
  13.8 5.3 %all-to-all-start = ((s32[4,1,4,1]{2,3,1,0:T(1,128)}), s32[4,1,4,1]{2,3,1,0:T(1,128)S(1)}, u32[]{:S(2)}, u32[]{:S(2)}) async-start(s32[4,1,4,1]{2,3,1,0:T(1,128)} %pad_add_fusion), calls=%async_computation | async-start | bytes 4096 | tf_op jit(solution)/shard_map/all_to_all | solution.py:17
  19.1 1.5 %slice_select_fusion = bf16[256,192]{0,1:T(8,128)(2,1)} fusion(bf16[512,192]{0,1:T(8,128)(2,1)S(1)} %copy-done.2, bf16[1024,192]{0,1:T(8,128)(2,1)} %param.11, pred[]{:T(512)S(6)} %eq.11), kind=kLoop, calls=%fused_computation.60 | loop fusion | flops 49152 | bytes 294913 | tf_op jit(solution)/shard_map/jit(_where)/select_n | solution.py:161
  20.7 2.0 %collective-permute-start.4 = (bf16[256,192]{0,1:T(8,128)(2,1)}, bf16[256,192]{0,1:T(8,128)(2,1)}, u32[]{:S(2)}, u32[]{:S(2)}) collective-permute-start(bf16[256,192]{0,1:T(8,128)(2,1)} %slice_select_fusion), channel_id=1, source_target_pairs={{0,8},{8,16},{16,24},{24,0},{1,9},{9,17},{17,25},{25,1},{2,10},{10... | collective-permute-start | bytes 294920 | tf_op jit(solution)/shard_map/ppermute | solution.py:24
  26.6 0.7 add.275
  29.5 0.7 copy.64
  30.2 0.7 copy.79
  31.5 0.7 copy.68
  34.3 0.7 gather_fusion.4
  35.1 0.8 broadcast_select_fusion
  35.9 0.7 copy.77
  36.6 3.6 %all-to-all-start.2 = ((bf16[1,4,4,64,128]{4,3,1,0,2:T(8,128)(2,1)}), bf16[1,4,4,64,128]{4,3,1,0,2:T(8,128)(2,1)S(1)}, u32[]{:S(2)}, u32[]{:S(2)}) async-start(bf16[1,4,4,64,128]{4,3,1,0,2:T(8,128)(2,1)} %copy.77), calls=%async_computation.2 | async-start | bytes 524288 | tf_op jit(solution)/shard_map/all_to_all | solution.py:156
  40.2 1.6 %copy_select_fusion = bf16[1,4,4,64,192]{4,3,1,0,2:T(8,128)(2,1)} fusion(bf16[1,4,4,64,192]{4,3,2,1,0:T(8,128)(2,1)S(1)} %bitcast.105, bf16[1,4,4,64,192]{4,3,2,1,0:T(8,128)(2,1)S(1)} %bitcast.104, pred[4,4]{0,1:T(4,128)(4,1)} %bitcast.117), kind=kLoop, calls=%fused_computation.44 | loop fusion | flops 196608 | bytes 1179664 | tf_op jit(solution)/shard_map/jit(_where)/select_n | solution.py:144
  41.8 2.0 %collective-permute-start.5 = (bf16[256,128]{1,0:T(8,128)(2,1)S(1)}, bf16[256,128]{1,0:T(8,128)(2,1)S(1)}, u32[]{:S(2)}, u32[]{:S(2)}) collective-permute-start(bf16[256,128]{1,0:T(8,128)(2,1)S(1)} %copy-done.6), channel_id=1, source_target_pairs={{0,8},{8,16},{16,24},{24,0},{1,9},{9,17},{17,25},{25,1},{2,10},{10... | collective-permute-start | bytes 196616 | tf_op jit(solution)/shard_map/ppermute | solution.py:24
  43.8 0.7 maximum_convert_fusion.2
  44.6 0.7 maximum_convert_fusion.3
  45.7 13.2 %all_gather.7 = bf16[384,128]{1,0:T(8,128)(2,1)S(1)} all-gather(bf16[96,128]{1,0:T(8,128)(2,1)S(1)} %pad_maximum_fusion.1), channel_id=1, replica_groups=mesh['parts'=1,'ctx'=4,'pb'=4,'row'=2] {'ctx'}, dimensions={0}, use_global_device_ids=true | all-gather | bytes 122880 | tf_op jit(solution)/shard_map/all_gather | solution.py:103
  59.0 0.8 maximum_convert_fusion
  60.0 0.7 maximum_convert_fusion.1
  61.7 13.6 %all_gather.6 = bf16[384,192]{1,0:T(8,128)(2,1)S(1)} all-gather(bf16[96,192]{1,0:T(8,128)(2,1)S(1)} %pad_maximum_fusion), channel_id=1, replica_groups=mesh['parts'=1,'ctx'=4,'pb'=4,'row'=2] {'ctx'}, dimensions={0}, use_global_device_ids=true | all-gather | bytes 184320 | tf_op jit(solution)/shard_map/all_gather | solution.py:102
  76.0 0.7 fusion.5
  76.8 3.7 %all-to-all-start.1 = ((bf16[1,4,4,64,192]{4,3,1,0,2:T(8,128)(2,1)}), bf16[1,4,4,64,192]{4,3,1,0,2:T(8,128)(2,1)S(1)}, u32[]{:S(2)}, u32[]{:S(2)}) async-start(bf16[1,4,4,64,192]{4,3,1,0,2:T(8,128)(2,1)} %copy_select_fusion), calls=%async_computation.1 | async-start | bytes 1048576 | tf_op jit(solution)/shard_map/all_to_all | solution.py:155
  80.5 1.7 %fusion.59 = (f32[1024]{0:T(1024)S(1)}, f32[1024,320]{0,1:T(8,128)S(1)}) fusion(bf16[1024,192]{1,0:T(8,128)(2,1)S(1)} %reshape.324, s32[]{:T(128)S(6)} %select_n.217, bf16[256,192]{0,1:T(8,128)(2,1)} %collective-permute-done.4, bf16[512,192]{0,1:T(8,128)(2,1)S(1)} %copy-done.2, s32[1024]{0:T(1024)S(1)} %copy-done.10, s32[1024]{0:T(1024)S(1)} %copy-done.7, ...), kind=kOutput, calls=%fused_computation.143 | convolution fusion | flops 128039936 | bytes 2012420 | tf_op jit(solution)/shard_map/dot_general | solution.py:37
  83.4 7.2 %all-to-all-done.1 = bf16[1,4,4,64,192]{4,3,1,0,2:T(8,128)(2,1)S(1)} async-done(((bf16[1,4,4,64,192]{4,3,1,0,2:T(8,128)(2,1)}), bf16[1,4,4,64,192]{4,3,1,0,2:T(8,128)(2,1)S(1)}, u32[]{:S(2)}, u32[]{:S(2)}) %all-to-all-start.1) | async-done | bytes 393248 | tf_op jit(solution)/shard_map/all_to_all | solution.py:155
  90.6 1.2 %fusion = (f32[1024]{0:T(1024)S(1)}, f32[1024,1024]{1,0:T(8,128)S(1)}) fusion(s32[1024]{0:T(1024)S(1)} %copy-done.7, s32[1024]{0:T(1024)S(1)} %copy-done.9, pred[1024]{0:T(1024)(128)(4,1)S(1)} %copy-done.17, bf16[1024,192]{1,0:T(8,128)(2,1)S(1)} %bitcast.113, bf16[1024,192]{1,0:T(8,128)(2,1)S(1)} %reshape.324), kind=kOutput, calls=%fused_computation.8 | convolution fusion | flops 407895040 | bytes 4994048 | tf_op jit(solution)/shard_map/dot_general | solution.py:37
  91.9 1.9 %fusion.52 = f32[1024]{0:T(1024)S(1)} fusion(f32[1024]{0:T(1024)S(1)} %get-tuple-element.34, f32[1024,1024]{1,0:T(8,128)S(1)} %get-tuple-element.35, s32[1024]{0:T(1024)S(1)} %copy-done.7, s32[1024]{0:T(1024)S(1)} %copy-done.9, pred[1024]{0:T(1024)(128)(4,1)S(1)} %copy-done.17), kind=kLoop, calls=%fused_computation.136 | loop fusion | flops 7339008 | bytes 4211712 | tf_op jit(solution)/shard_map/reduce_sum | solution.py:43
  93.8 1.8 %fusion.6 = f32[1024,128]{1,0:T(8,128)S(1)} fusion(bf16[1024,128]{1,0:T(8,128)(2,1)S(1)} %bitcast.114, f32[1024]{0:T(1024)S(1)} %fusion.52, f32[1024,1024]{1,0:T(8,128)S(1)} %get-tuple-element.35, f32[1024]{0:T(1024)S(1)} %get-tuple-element.34, s32[1024]{0:T(1024)S(1)} %copy-done.7, s32[1024]{0:T(1024)S(1)} %copy-done.9, pred[1024]{0:T(1024)(128)(4,1)S(1)} %copy-done.17), kind=kOutput, calls=%fused_computation.20 | convolution fusion | flops 275906560 | bytes 4998144 | tf_op jit(solution)/shard_map/dot_general | solution.py:42
  96.8 1.3 %fusion.25 = bf16[64,2048]{1,0:T(8,128)(2,1)} fusion(f32[64,2048]{1,0:T(8,128)S(1)} %reshape.332, f32[8,8,16,128]{3,2,1,0:T(8,128)S(1)} %bitcast.108, f32[64,2048]{1,0:T(8,128)S(1)} %reshape.331, f32[8,8,16,128]{3,2,1,0:T(8,128)S(1)} %bitcast.107, f32[64,2048]{1,0:T(8,128)S(1)} %reshape.325, f32[8,8,16,128]{3,2,1,0:T(8,128)S(1)} %bitcast.106), kind=kLoop, calls=%fused_computation.40 | loop fusion | flops 786432 | bytes 3407872 | tf_op jit(solution)/shard_map/convert_element_type | solution.py:196
  (120 shorter events, 16.7 us)
Async XLA Ops:
  0.0 19.1 %copy-start.2 = (bf16[512,192]{0,1:T(8,128)(2,1)S(1)}, bf16[512,192]{0,1:T(8,128)(2,1)}, u32[]{:S(2)}) copy-start(bf16[512,192]{0,1:T(8,128)(2,1)} %param.13) | copy-start | bytes 589828
  0.0 25.2 %copy-start.1 = (bf16[1024,128]{1,0:T(8,128)(2,1)S(1)}, bf16[1024,128]{1,0:T(8,128)(2,1)}, u32[]{:S(2)}) copy-start(bf16[1024,128]{1,0:T(8,128)(2,1)} %param.12) | copy-start | bytes 786436
  0.0 25.2 %copy-start = (bf16[512,128]{1,0:T(8,128)(2,1)S(1)}, bf16[512,128]{1,0:T(8,128)(2,1)}, u32[]{:S(2)}) copy-start(bf16[512,128]{1,0:T(8,128)(2,1)} %param.14) | copy-start | bytes 393220
  0.0 25.8 %copy-start.8 = (f32[32,192]{1,0:T(8,128)S(1)}, f32[32,192]{1,0:T(8,128)}, u32[]{:S(2)}) copy-start(f32[32,192]{1,0:T(8,128)} %param.15) | copy-start | bytes 73732
  0.0 25.8 %copy-start.3 = (bf16[64,3072]{1,0:T(8,128)(2,1)S(1)}, bf16[64,3072]{1,0:T(8,128)(2,1)}, u32[]{:S(2)}) copy-start(bf16[64,3072]{1,0:T(8,128)(2,1)} %param.10) | copy-start | bytes 1179652
  0.0 26.4 %copy-start.13 = (f32[32,128]{1,0:T(8,128)S(1)}, f32[32,128]{1,0:T(8,128)}, u32[]{:S(2)}) copy-start(f32[32,128]{1,0:T(8,128)} %param.16) | copy-start | bytes 49156
  0.0 29.4 %copy-start.14 = (bf16[64,48]{0,1:T(8,128)(2,1)S(1)}, bf16[64,48]{0,1:T(8,128)(2,1)}, u32[]{:S(2)}) copy-start(bf16[64,48]{0,1:T(8,128)(2,1)} %param.17) | copy-start | bytes 18436
  3.0 56.0 %collective-permute-start = (bf16[16,192]{1,0:T(8,128)(2,1)}, bf16[16,192]{1,0:T(8,128)(2,1)}, u32[]{:S(2)}, u32[]{:S(2)}) collective-permute-start(bf16[16,192]{1,0:T(8,128)(2,1)} %get-tuple-element.17), channel_id=1, source_target_pairs={{0,24},{8,0},{16,8},{24,16},{1,25},{9,1},{17,9},{25,17},{2,26},{10... | collective-permute-start | bytes 18440 | tf_op jit(solution)/shard_map/ppermute | solution.py:24
  8.1 51.9 %collective-permute-start.1 = (bf16[16,192]{1,0:T(8,128)(2,1)}, bf16[16,192]{1,0:T(8,128)(2,1)}, u32[]{:S(2)}, u32[]{:S(2)}) collective-permute-start(bf16[16,192]{1,0:T(8,128)(2,1)} %get-tuple-element.18), channel_id=1, source_target_pairs={{0,24},{8,0},{16,8},{24,16},{1,25},{9,1},{17,9},{25,17},{2,26},{10... | collective-permute-start | bytes 18440 | tf_op jit(solution)/shard_map/ppermute | solution.py:24
  9.8 32.0 %collective-permute-start.2 = (bf16[16,128]{1,0:T(8,128)(2,1)}, bf16[16,128]{1,0:T(8,128)(2,1)}, u32[]{:S(2)}, u32[]{:S(2)}) collective-permute-start(bf16[16,128]{1,0:T(8,128)(2,1)} %get-tuple-element.19), channel_id=1, source_target_pairs={{0,24},{8,0},{16,8},{24,16},{1,25},{9,1},{17,9},{25,17},{2,26},{10... | collective-permute-start | bytes 12296 | tf_op jit(solution)/shard_map/ppermute | solution.py:24
  10.3 34.3 %collective-permute-start.3 = (bf16[16,128]{1,0:T(8,128)(2,1)}, bf16[16,128]{1,0:T(8,128)(2,1)}, u32[]{:S(2)}, u32[]{:S(2)}) collective-permute-start(bf16[16,128]{1,0:T(8,128)(2,1)} %get-tuple-element.20), channel_id=1, source_target_pairs={{0,24},{8,0},{16,8},{24,16},{1,25},{9,1},{17,9},{25,17},{2,26},{10... | collective-permute-start | bytes 12296 | tf_op jit(solution)/shard_map/ppermute | solution.py:24
  13.8 17.0 %all-to-all-start = ((s32[4,1,4,1]{2,3,1,0:T(1,128)}), s32[4,1,4,1]{2,3,1,0:T(1,128)S(1)}, u32[]{:S(2)}, u32[]{:S(2)}) async-start(s32[4,1,4,1]{2,3,1,0:T(1,128)} %pad_add_fusion), calls=%async_computation | async-start | bytes 4096 | tf_op jit(solution)/shard_map/all_to_all | solution.py:17
  20.7 59.9 %collective-permute-start.4 = (bf16[256,192]{0,1:T(8,128)(2,1)}, bf16[256,192]{0,1:T(8,128)(2,1)}, u32[]{:S(2)}, u32[]{:S(2)}) collective-permute-start(bf16[256,192]{0,1:T(8,128)(2,1)} %slice_select_fusion), channel_id=1, source_target_pairs={{0,8},{8,16},{16,24},{24,0},{1,9},{9,17},{17,25},{25,1},{2,10},{10... | collective-permute-start | bytes 294920 | tf_op jit(solution)/shard_map/ppermute | solution.py:24
  32.6 1.8 %copy-start.12 = (s32[1024]{0:T(1024)}, s32[1024]{0:T(1024)S(1)}, u32[]{:S(2)}) copy-start(s32[1024]{0:T(1024)S(1)} %pad_clamp_fusion) | copy-start | bytes 12292
  35.9 5.9 %copy-start.6 = (bf16[256,128]{1,0:T(8,128)(2,1)S(1)}, bf16[256,128]{1,0:T(8,128)(2,1)}, u32[]{:S(2)}) copy-start(bf16[256,128]{1,0:T(8,128)(2,1)} %slice_select_fusion.1) | copy-start | bytes 196612
  36.6 40.2 %all-to-all-start.2 = ((bf16[1,4,4,64,128]{4,3,1,0,2:T(8,128)(2,1)}), bf16[1,4,4,64,128]{4,3,1,0,2:T(8,128)(2,1)S(1)}, u32[]{:S(2)}, u32[]{:S(2)}) async-start(bf16[1,4,4,64,128]{4,3,1,0,2:T(8,128)(2,1)} %copy.77), calls=%async_computation.2 | async-start | bytes 524288 | tf_op jit(solution)/shard_map/all_to_all | solution.py:156
  41.8 40.8 %collective-permute-start.5 = (bf16[256,128]{1,0:T(8,128)(2,1)S(1)}, bf16[256,128]{1,0:T(8,128)(2,1)S(1)}, u32[]{:S(2)}, u32[]{:S(2)}) collective-permute-start(bf16[256,128]{1,0:T(8,128)(2,1)S(1)} %copy-done.6), channel_id=1, source_target_pairs={{0,8},{8,16},{16,24},{24,0},{1,9},{9,17},{17,25},{25,1},{2,10},{10... | collective-permute-start | bytes 196616 | tf_op jit(solution)/shard_map/ppermute | solution.py:24
  60.8 14.4 %copy-start.11 = (s32[1024]{0:T(1024)S(1)}, s32[1024]{0:T(1024)}, u32[]{:S(2)}) copy-start(s32[1024]{0:T(1024)} %broadcast_add_fusion.1) | copy-start | bytes 12292
  60.8 14.4 %copy-start.16 = (s32[384]{0:T(512)S(1)}, s32[384]{0:T(512)}, u32[]{:S(2)}) copy-start(s32[384]{0:T(512)} %multiply_add_fusion) | copy-start | bytes 4612
  76.7 3.8 %copy-start.7 = (s32[1024]{0:T(1024)S(1)}, s32[1024]{0:T(1024)}, u32[]{:S(2)}) copy-start(s32[1024]{0:T(1024)} %fusion.31) | copy-start | bytes 12292
  76.7 3.8 %copy-start.10 = (s32[1024]{0:T(1024)S(1)}, s32[1024]{0:T(1024)}, u32[]{:S(2)}) copy-start(s32[1024]{0:T(1024)} %broadcast_add_fusion) | copy-start | bytes 12292
  76.7 3.8 %copy-start.15 = (s32[320]{0:T(512)S(1)}, s32[320]{0:T(512)}, u32[]{:S(2)}) copy-start(s32[320]{0:T(512)} %iota_add_fusion.1) | copy-start | bytes 3844
  76.8 13.7 %all-to-all-start.1 = ((bf16[1,4,4,64,192]{4,3,1,0,2:T(8,128)(2,1)}), bf16[1,4,4,64,192]{4,3,1,0,2:T(8,128)(2,1)S(1)}, u32[]{:S(2)}, u32[]{:S(2)}) async-start(bf16[1,4,4,64,192]{4,3,1,0,2:T(8,128)(2,1)} %copy_select_fusion), calls=%async_computation.1 | async-start | bytes 1048576 | tf_op jit(solution)/shard_map/all_to_all | solution.py:155
  83.3 7.3 %copy-start.9 = (s32[1024]{0:T(1024)S(1)}, s32[1024]{0:T(1024)}, u32[]{:S(2)}) copy-start(s32[1024]{0:T(1024)} %add.275) | copy-start | bytes 12292
  83.3 7.3 %copy-start.17 = (pred[1024]{0:T(1024)(128)(4,1)S(1)}, pred[1024]{0:T(1024)(128)(4,1)}, u32[]{:S(2)}) copy-start(pred[1024]{0:T(1024)(128)(4,1)} %and.99) | copy-start | bytes 3076
  95.6 0.8 copy-start.4
  95.6 0.9 copy-start.5
